TPU v7x, 768 devices: a whole 4x8x12 slice. The times are simulated.
768 devices in a mesh: dp: 16 (over x, y_hi), pipe: 12 (over z), tensor: 4 (over y_lo, core).
Axes of the slice: x: 4, y: 8 (y_hi: 4, y_lo: 2; y = y_hi * 2 + y_lo), z: 12, core: 2. Of those that a mesh axis runs over, the one named last changes fastest.
Arguments:
- x_stash: bfloat16 [12, 2, 8192, 1536], P('pipe', None, ('dp', 'tensor'))
- h_stash: bfloat16 [12, 2, 8192, 3072], P('pipe', None, 'dp', 'tensor'), may hold values from -8 to 8
- cotangent: bfloat16 [12, 8192, 1536], P('pipe', ('dp', 'tensor')), may hold values from -16 to 16
- plan: int32 [12], P('pipe'), may hold values from 0 to 1, as said below
- conv_w: float32 [12, 7, 1536], P('pipe'), may hold values from -2 to 2
- conv_b: float32 [12, 1536], P('pipe'), may hold values from -5 to 5
- norm_gain: float32 [12, 1536], P('pipe'), may hold values from 0.1 to 1.9
- shift_b: float32 [12, 1536], P('pipe'), may hold values from -3 to 3
- w_in: bfloat16 [12, 1536, 3072], P('pipe', None, 'tensor'), may hold values from -0.15625 to 0.15625
- w_out: bfloat16 [12, 3072, 1536], P('pipe', 'tensor'), may hold values from -0.109375 to 0.109375
Outputs:
- grad_in: bfloat16 [12, 8192, 1536], P('pipe', ('dp', 'tensor'))
- grad_w_in: float32 [12, 1536, 3072], P('pipe', 'dp', 'tensor')
- grad_w_out: float32 [12, 3072, 1536], P('pipe', 'tensor', 'dp')
- grad_conv: float32 [12, 8, 1536], P('pipe')
- grad_affine: float32 [12, 3, 1536], P('pipe')
- grad_b_in: float32 [12, 3072], P('pipe')
Inputs may be any that keep to these rules, and one draw needn't show every extreme that they name: `plan`: each of the 2 stashed microbatches is taken by some section.
All inputs are finite; a program needn't handle non-finite values.
Results may differ from a plain program's by a relative error of at most 0.017.
Values may be sent and summed in bfloat16 or wider, within the bound.
A program may use at most 64 MiB of HBM per device.

v0:
```python
import math

import jax
import jax.numpy as jnp
from jax import lax
from jax.sharding import PartitionSpec as P

gelu_coef = 0.044715
root_coef = math.sqrt(2.0 / math.pi)
norm_eps = 1e-06


def extended(block, sides, width):
    for axis, dim in sides:
        count = lax.axis_size(axis)
        forward = [(i, i + 1) for i in range(count - 1)]
        backward = [(target, source) for source, target in forward]
        low = lax.ppermute(
            lax.slice_in_dim(block, block.shape[dim] - width, None, axis=dim), axis, forward
        )
        high = lax.ppermute(lax.slice_in_dim(block, 0, width, axis=dim), axis, backward)
        block = jnp.concatenate([low, block, high], axis=dim)
    return block


def shifted(x, axis, by):
    size = lax.axis_size(axis)
    pairs = [(i, i + by) for i in range(size) if 0 <= i + by < size]
    return lax.ppermute(x, axis, pairs)


def gelu_pair(hidden):
    inner_arg = root_coef * (hidden + gelu_coef * hidden * hidden * hidden)
    tangent = jnp.tanh(inner_arg)
    gelu_value = 0.5 * hidden * (1.0 + tangent)
    gelu_slope = 0.5 * (1.0 + tangent) + 0.5 * hidden * (1.0 - tangent * tangent) * root_coef * (
        1.0 + 3.0 * gelu_coef * hidden * hidden
    )
    return (gelu_value, gelu_slope)


def rim_norm(x_wide, kernel_w, kernel_b, gain_v, shift_v, extent):
    kernel = kernel_w.shape[0]
    wide_f = x_wide.astype(jnp.float32)
    conv_out = kernel_b + sum(
        (
            kernel_w[kernel_tap] * wide_f[kernel_tap : kernel_tap + extent]
            for kernel_tap in range(kernel)
        )
    )
    center = conv_out - jnp.mean(conv_out, -1, keepdims=True)
    inv_std = lax.rsqrt(jnp.mean(center * center, -1, keepdims=True) + norm_eps)
    normed = center * inv_std
    scaled = (normed * gain_v + shift_v).astype(jnp.bfloat16)
    return (wide_f, normed, inv_std, scaled)


def contract_rows(first_side, second_side):
    return lax.dot_general(
        first_side, second_side, (((0,), (0,)), ((), ())), preferred_element_type=jnp.float32
    )


def contract_cols(first_side, second_side):
    return lax.dot_general(
        first_side, second_side, (((1,), (1,)), ((), ())), preferred_element_type=jnp.float32
    )


def per_device(x_stash, h_stash, cotangent, plan, conv_w, conv_b, norm_gain, shift_b, w_in, w_out):
    stash_slot = plan[0]
    x_rows = lax.dynamic_index_in_dim(x_stash[0], stash_slot, 0, keepdims=False)
    h_local = lax.dynamic_index_in_dim(h_stash[0], stash_slot, 0, keepdims=False)
    g_rows = cotangent[0]
    tensor_count = lax.axis_size("tensor")
    tok_rows = x_rows.shape[0]
    kernel_w = conv_w[0]
    gain_v = norm_gain[0]
    kernel = kernel_w.shape[0]
    margin = kernel // 2
    extent = tok_rows + 2 * margin
    x_wide = extended(x_rows, (("tensor", 0),), 2 * margin)
    wide_f, normed_ext, inv_ext, scaled_ext = rim_norm(
        x_wide, kernel_w, conv_b[0], gain_v, shift_b[0], extent
    )
    scaled_own = scaled_ext[margin : margin + tok_rows]
    scaled, g_full = (
        lax.all_gather(scaled_own, "tensor", axis=0, tiled=True),
        lax.all_gather(g_rows, "tensor", axis=0, tiled=True),
    )
    gelu_value, gelu_slope = gelu_pair(h_local.astype(jnp.float32))
    active = gelu_value.astype(jnp.bfloat16)
    d_act = contract_cols(g_full, w_out[0])
    d_hidden = d_act * gelu_slope
    d_hidden_b = d_hidden.astype(jnp.bfloat16)
    weight_part = jnp.stack([contract_rows(scaled, d_hidden_b), contract_rows(g_full, active)], 1)
    summed = lax.psum_scatter(
        weight_part.astype(jnp.bfloat16), "dp", scatter_dimension=0, tiled=True
    ).astype(jnp.float32)
    d_part = contract_cols(d_hidden_b, w_in[0])
    d_padded = jnp.pad(d_part, ((margin, margin), (0, 0)))
    blocks = jnp.stack(
        [
            d_padded[block_index * tok_rows : block_index * tok_rows + extent]
            for block_index in range(tensor_count)
        ]
    )
    d_scaled = lax.psum_scatter(
        blocks.astype(jnp.bfloat16), "tensor", scatter_dimension=0, tiled=True
    ).astype(jnp.float32)[0]
    d_normed = d_scaled * gain_v
    d_mixed = inv_ext * (
        d_normed
        - jnp.mean(d_normed, -1, keepdims=True)
        - normed_ext * jnp.mean(d_normed * normed_ext, -1, keepdims=True)
    )
    d_scaled_own = d_scaled[margin : margin + tok_rows]
    normed_own = normed_ext[margin : margin + tok_rows]
    d_mixed_own = d_mixed[margin : margin + tok_rows]
    grad_gain = jnp.sum(d_scaled_own * normed_own, 0)
    grad_shift = jnp.sum(d_scaled_own, 0)
    grad_convb = jnp.sum(d_mixed_own, 0)
    grad_convw = jnp.stack(
        [
            jnp.sum(d_mixed_own * wide_f[margin + kernel_tap : margin + kernel_tap + tok_rows], 0)
            for kernel_tap in range(kernel)
        ]
    )
    d_input = sum(
        (
            kernel_w[kernel_tap]
            * d_mixed[2 * margin - kernel_tap : 2 * margin - kernel_tap + tok_rows]
            for kernel_tap in range(kernel)
        )
    )
    grad_x = (g_rows.astype(jnp.float32) + d_input).astype(jnp.bfloat16)
    grad_bout = jnp.sum(g_rows.astype(jnp.float32), 0)
    hidden_local = h_local.shape[1]
    bias_in = lax.dynamic_update_slice_in_dim(
        jnp.zeros((hidden_local * tensor_count,), jnp.float32),
        jnp.sum(d_hidden, 0),
        lax.axis_index("tensor") * hidden_local,
        0,
    )
    conv_grad = jnp.concatenate([grad_convw, grad_convb[None]], 0)
    affine_grad = jnp.stack([grad_gain, grad_shift, grad_bout])
    conv_sum, affine_sum, bias_sum = lax.psum((conv_grad, affine_grad, bias_in), ("dp", "tensor"))
    grad_in = shifted(grad_x, "pipe", -1)
    return (
        grad_in[None],
        summed[:, 0, :][None],
        summed[:, 1, :].T[None],
        conv_sum[None],
        affine_sum[None],
        bias_sum[None],
    )


def solution(mesh):
    return jax.shard_map(
        per_device,
        mesh=mesh,
        in_specs=(
            P("pipe", None, ("dp", "tensor"), None),
            P("pipe", None, "dp", "tensor"),
            P("pipe", ("dp", "tensor"), None),
            P("pipe"),
            P("pipe", None, None),
            P("pipe", None),
            P("pipe", None),
            P("pipe", None),
            P("pipe", None, "tensor"),
            P("pipe", "tensor", None),
        ),
        out_specs=(
            P("pipe", ("dp", "tensor"), None),
            P("pipe", "dp", "tensor"),
            P("pipe", "tensor", "dp"),
            P("pipe", None, None),
            P("pipe", None, None),
            P("pipe", None),
        ),
        check_vma=False,
    )
```

profile of v0, /device:TPU:1, one launch (start us, length us, event | category | flops | bytes accessed | tf_op | source)
XLA Modules:
  0.0 453.4 jit_solution(7565366376722505201)
XLA Ops:
  7.2 0.0 all-gather.6.cloned.1.call-start
  7.2 0.7 all-gather.6.cloned.1.call-update
  7.9 0.0 reduce-scatter.3.cloned.1.call-start
  8.6 42.7 %all-gather.6.cloned.1.call-done = bf16[1,512,1536]{2,1,0:T(8,128)(2,1)} async-done(((bf16[1,128,1536]{2,1,0:T(8,128)(2,1)}), bf16[1,512,1536]{2,1,0:T(8,128)(2,1)}) %all-gather.6.cloned.1.call-update) | async-done | bytes 1572880 | tf_op jit(solution)/shard_map/all_gather | solution.py:89
  51.3 4.4 fusion.64
  55.7 1.4 fusion.2
  57.2 0.4 fusion.53
  57.5 1.4 pad_maximum_fusion.1
  59.0 0.0 all-gather.4.cloned.1.call-start
  59.0 1.0 copy-done.8
  60.1 1.9 collective-permute-start
  62.0 2.4 collective-permute-start.1
  64.4 0.8 dynamic-slice_bitcast_fusion
  65.2 0.1 slice_reduce_fusion.8
  65.5 1.7 collective-permute-done.1
  67.2 1.1 maximum_convert_fusion
  68.3 0.9 fusion.62
  69.2 0.9 copy-done.1
  70.1 0.2 multiply_reduce_fusion.1
  70.3 21.9 %reduce-scatter.3.cloned.1.call-done = bf16[1,134,1536]{2,1,0:T(8,128)(2,1)} async-done(((bf16[4,134,1536]{2,1,0:T(8,128)(2,1)}), bf16[1,134,1536]{2,1,0:T(8,128)(2,1)}) %reduce-scatter.3.cloned.1.call-update) | async-done | bytes 411664 | tf_op jit(solution)/shard_map/reduce_scatter | solution.py:108
  92.2 1.2 convert_element_type.40
  93.4 0.1 copy-done.2
  93.5 1.6 fusion.51
  95.1 0.9 copy-done.3
  96.0 1.0 fusion.45
  97.0 0.0 reduce-scatter.5.cloned.1.call-start
  97.0 4.6 %fusion.1 = bf16[1536,1,768]{2,0,1:T(8,128)(2,1)} fusion(bf16[1,512,1536]{2,1,0:T(8,128)(2,1)} %all-gather.6.cloned.1.call-done, bf16[1,2,512,768]{3,2,1,0:T(8,128)(2,1)} %param.11, s32[]{:T(128)S(6)} %select_n.9), kind=kOutput, calls=%fused_computation.11 | convolution fusion | flops 1213071360 | bytes 4718596 | tf_op jit(solution)/shard_map/dot_general | solution.py:59
  101.7 29.0 %all-gather.4.cloned.1.call-done = bf16[512,1536]{1,0:T(8,128)(2,1)} async-done(((bf16[128,1536]{1,0:T(8,128)(2,1)}), bf16[512,1536]{1,0:T(8,128)(2,1)}) %all-gather.4.cloned.1.call-update) | async-done | bytes 1572880 | tf_op jit(solution)/shard_map/all_gather | solution.py:88
  130.6 3.2 fusion
  133.8 2.5 pad_maximum_fusion
  136.4 0.0 all-reduce.4.cloned.1.call-start
  136.4 1.1 convert_reduce_fusion
  137.6 1.5 subtract_multiply_fusion
  139.1 1.5 fusion.31
  140.6 1.4 collective-permute-start.2
  142.0 0.8 fusion.32
  142.9 0.1 slice_reduce_fusion
  143.1 0.6 broadcast_in_dim.29
  143.7 0.7 concatenate.7
  144.4 9.0 %collective-permute-done.2 = bf16[128,1536]{1,0:T(8,128)(2,1)} collective-permute-done((bf16[128,1536]{1,0:T(8,128)(2,1)}, bf16[128,1536]{1,0:T(8,128)(2,1)}, u32[]{:S(2)}, u32[]{:S(2)}) %collective-permute-start.2) | collective-permute-done | bytes 393248 | tf_op jit(solution)/shard_map/ppermute | solution.py:29
  153.4 92.4 %reduce-scatter.5.cloned.1.call-done = bf16[96,2,768]{2,0,1:T(8,128)(2,1)} async-done(((bf16[1536,2,768]{2,0,1:T(8,128)(2,1)}), bf16[96,2,768]{2,0,1:T(8,128)(2,1)}) %reduce-scatter.5.cloned.1.call-update) | async-done | bytes 294928 | tf_op jit(solution)/shard_map/reduce_scatter | solution.py:97
  245.9 1.0 convert_element_type.44
  246.9 0.8 slice_bitcast_fusion.2
  247.7 193.3 %all-reduce.4.cloned.1.call-done = (f32[1,8,1536]{2,1,0:T(8,128)}, f32[1,3,1536]{2,0,1:T(1,128)}, f32[1,3072]{1,0:T(1,128)}) async-done(((f32[1,8,1536]{2,1,0:T(8,128)}, f32[1,3,1536]{2,0,1:T(1,128)}, f32[1,3072]{1,0:T(1,128)}), (f32[1,8,1536]{2,1,0:T(8,128)}, f32[1,3,1536]{2,0,1:T(1,128)}, f32[1,3072]{1,0:T(1,128)})) %all-reduce.4.cloned.1.call-update) | async-done | bytes 79888 | tf_op jit(solution)/shard_map/psum | solution.py:147
  441.0 1.8 copy.24
  442.8 1.4 copy.25
  444.2 1.3 copy.26
  445.6 1.3 copy.27
  (52 shorter events, 0.3 us)
Async XLA Ops:
  7.2 48.5 %copy-start = (bf16[1,1536,768]{2,1,0:T(8,128)(2,1)S(1)}, bf16[1,1536,768]{2,1,0:T(8,128)(2,1)}, u32[]{:S(2)}) copy-start(bf16[1,1536,768]{2,1,0:T(8,128)(2,1)} %param.18) | copy-start | bytes 7077892
  7.2 44.1 %all-gather.6.cloned.1.call-start = ((), (), s32[]{:S(2)}) async-start(), calls=%async_computation.5 | async-start | bytes 1966080 | tf_op jit(solution)/shard_map/all_gather | solution.py:89
  7.9 84.3 %reduce-scatter.3.cloned.1.call-start = ((), (), s32[]{:S(2)}) async-start(), calls=%async_computation.2 | async-start | bytes 2088960 | tf_op jit(solution)/shard_map/reduce_scatter | solution.py:108
  55.7 1.4 copy-start.14
  58.9 1.1 copy-start.8
  58.9 6.3 %copy-start.10 = (f32[1,7,1536]{2,0,1:T(1,128)S(1)}, f32[1,7,1536]{2,0,1:T(1,128)}, u32[]{:S(2)}) copy-start(f32[1,7,1536]{2,0,1:T(1,128)} %param.14) | copy-start | bytes 129028
  59.0 6.4 %copy-start.11 = (f32[1,1536]{1,0:T(1,128)S(1)}, f32[1,1536]{1,0:T(1,128)}, u32[]{:S(2)}) copy-start(f32[1,1536]{1,0:T(1,128)} %param.16) | copy-start | bytes 18436
  59.0 6.4 %copy-start.12 = (f32[1,1536]{1,0:T(1,128)S(1)}, f32[1,1536]{1,0:T(1,128)}, u32[]{:S(2)}) copy-start(f32[1,1536]{1,0:T(1,128)} %param.15) | copy-start | bytes 18436
  59.0 6.5 %copy-start.13 = (f32[1,1536]{1,0:T(1,128)S(1)}, f32[1,1536]{1,0:T(1,128)}, u32[]{:S(2)}) copy-start(f32[1,1536]{1,0:T(1,128)} %param.17) | copy-start | bytes 18436
  59.0 71.6 %all-gather.4.cloned.1.call-start = ((), (), s32[]{:S(2)}) async-start(), calls=%async_computation.3 | async-start | bytes 1966080 | tf_op jit(solution)/shard_map/all_gather | solution.py:88
  60.1 5.4 %collective-permute-start = (bf16[6,1536]{1,0:T(8,128)(2,1)S(1)}, bf16[6,1536]{1,0:T(8,128)(2,1)S(1)}, u32[]{:S(2)}, u32[]{:S(2)}) collective-permute-start(bf16[6,1536]{1,0:T(8,128)(2,1)S(1)} %get-tuple-element.35), channel_id=1, source_target_pairs={{0,1},{1,2},{2,3},{4,5},{5,6},{6,7},{8,9},{9,10},{10,11},{12,13},{... | collective-permute-start | bytes 55304 | tf_op jit(solution)/shard_map/ppermute | solution.py:18
  62.0 5.1 %collective-permute-start.1 = (bf16[6,1536]{1,0:T(8,128)(2,1)S(1)}, bf16[6,1536]{1,0:T(8,128)(2,1)S(1)}, u32[]{:S(2)}, u32[]{:S(2)}) collective-permute-start(bf16[6,1536]{1,0:T(8,128)(2,1)S(1)} %get-tuple-element.36), channel_id=1, source_target_pairs={{1,0},{2,1},{3,2},{5,4},{6,5},{7,6},{9,8},{10,9},{11,10},{13,12},{... | collective-permute-start | bytes 55304 | tf_op jit(solution)/shard_map/ppermute | solution.py:21
  69.2 0.9 copy-start.1
  92.2 1.3 copy-start.2
  93.5 3.5 copy-start.4
  95.1 0.9 copy-start.3
  97.0 148.9 %reduce-scatter.5.cloned.1.call-start = ((), (), s32[]{:S(2)}) async-start(), calls=%async_computation.4 | async-start | bytes 5013504 | tf_op jit(solution)/shard_map/reduce_scatter | solution.py:97
  130.6 3.2 copy-start.7
  136.4 304.7 %all-reduce.4.cloned.1.call-start = ((), (), s32[]{:S(2)}) async-start(), calls=%async_computation.6 | async-start | bytes 159744 | tf_op jit(solution)/shard_map/psum | solution.py:147
  137.5 1.6 copy-start.6
  137.5 3.0 copy-start.9
  140.6 2.4 copy-start.5
  140.6 12.9 %collective-permute-start.2 = (bf16[128,1536]{1,0:T(8,128)(2,1)}, bf16[128,1536]{1,0:T(8,128)(2,1)}, u32[]{:S(2)}, u32[]{:S(2)}) collective-permute-start(bf16[128,1536]{1,0:T(8,128)(2,1)} %fusion.31), channel_id=1, source_target_pairs={{4,0},{8,4},{12,8},{16,12},{20,16},{24,20},{28,24},{32,28},{36,32}... | collective-permute-start | bytes 1179656 | tf_op jit(solution)/shard_map/ppermute | solution.py:29
Sparse Core Ops, SparseCore 0:
  10.4 40.8 all-gather.5
  59.1 33.0 reduce-scatter.2
  97.1 33.4 all-gather.3
  136.5 109.3 reduce-scatter.4
  250.1 190.9 all-reduce.3
where the time goes:
time: 454 us; the launch traced here: 453 us
  waiting for transfers between devices  391 us (86%)
  other arithmetic  15.9 us (4%)
  between operations  14.8 us (3%)
  matrix products  13.6 us (3%)
  local copies, waits for them, and re-layouts  12.4 us (3%)
  starting transfers between devices  5.94 us (1%)
    psum x1, waiting for transfers between devices, per_device(): lax.psum((conv_grad, affine_grad, bias_in), ('dp', 'tensor'))  193 us
    reduce_scatter x1, waiting for transfers between devices, per_device(): lax.psum_scatter(weight_part.astype(jnp.bfloat16), 'dp', scatter_dimensio...  92.4 us
    all_gather x1, waiting for transfers between devices, per_device(): lax.all_gather(g_rows, 'tensor', axis=0, tiled=True)  42.7 us
    all_gather x1, waiting for transfers between devices, per_device(): lax.all_gather(scaled_own, 'tensor', axis=0, tiled=True)  29 us
    reduce_scatter x1, waiting for transfers between devices, per_device(): lax.psum_scatter(blocks.astype(jnp.bfloat16), 'tensor', scatter_dimension...  21.9 us
  transfers between devices with their start and end apart: 8, of which 7 were waited for; matrix products, arithmetic and copies ran while one was open for 4% of the time, Pallas kernels for 0%

commit v1 on v0

v1 whole, which is shorter than its diff:
```python
import math

import jax
import jax.numpy as jnp
from jax import lax
from jax.experimental import pallas as pl
from jax.experimental.pallas import tpu as pltpu
from jax.sharding import PartitionSpec as P

MESH = pl.DeviceIdType.MESH
f32 = jnp.float32
bf16 = jnp.bfloat16

gelu_coef = 0.044715
root_coef = math.sqrt(2.0 / math.pi)
norm_eps = 1e-06

D = 1536
HID = 768
SEQ = 512
TOK = 128
KER = 7
CH = 384
XB = D // 4
YB = XB // 4
WIDE = TOK + 16
N_COPIES = 96
N_LOCAL = 16


def dot_tn(a, b):
    return lax.dot_general(a, b, (((0,), (0,)), ((), ())), preferred_element_type=f32)


def dot_nt(a, b):
    return lax.dot_general(a, b, (((1,), (1,)), ((), ())), preferred_element_type=f32)


def kernel(
    x_hbm, h_hbm, g_hbm, plan_ref, cw_ref, cb_ref, gain_ref, shift_ref, win_hbm, wout_hbm,
    gin_out, gwi_out, gwo_out, small_out,
    xs, hs, gf, sf, win, wout, halo, xw, normed, inv, active, slope, dh, dpart, s1, r1, s2, r2t,
    part, xr2, xrx, q, yr2, yrx, dmix, gx, accs, sm, arc, ar, arr, bias, ssem, rsem, lsem,
):
    dp = lax.axis_index("dp")
    pz = lax.axis_index("pipe")
    t = lax.axis_index("tensor")
    xi, yi = dp // 4, dp % 4
    ylo, core = t // 2, t % 2
    npipe = lax.axis_size("pipe")

    def dev(dp_=None, pz_=None, t_=None):
        return (
            dp if dp_ is None else dp_,
            pz if pz_ is None else pz_,
            t if t_ is None else t_,
        )

    core_dev = dev(t_=ylo * 2 + 1 - core)
    chip_dev = dev(t_=(t + 2) % 4)
    diag_dev = dev(t_=(1 - ylo) * 2 + 1 - core)
    seq_next, seq_prev = dev(t_=(t + 1) % 4), dev(t_=(t + 3) % 4)
    xp, xm = dev(dp_=((xi + 1) % 4) * 4 + yi), dev(dp_=((xi + 3) % 4) * 4 + yi)
    yp, ym = dev(dp_=xi * 4 + (yi + 1) % 4), dev(dp_=xi * 4 + (yi + 3) % 4)
    x_a = dev(dp_=(xi + 1 - 2 * (xi % 2)) * 4 + yi)
    x_b = dev(dp_=(3 - xi) * 4 + yi)
    y_a = dev(dp_=xi * 4 + yi + 1 - 2 * (yi % 2))
    y_b = dev(dp_=xi * 4 + 3 - yi)
    z_down = dev(pz_=(pz + npipe - 1) % npipe)
    z_up = dev(pz_=(pz + 1) % npipe)

    used = [0, 0]
    sent = []

    def remote(src, dst, to):
        i = used[0]
        used[0] += 1
        assert i < N_COPIES
        copy = pltpu.make_async_remote_copy(
            src_ref=src, dst_ref=dst, send_sem=ssem.at[i], recv_sem=rsem.at[i],
            device_id=to, device_id_type=MESH,
        )
        copy.start()
        sent.append(copy)
        return copy

    def local(src, dst):
        i = used[1]
        used[1] += 1
        assert i < N_LOCAL
        copy = pltpu.make_async_copy(src, dst, lsem.at[i])
        copy.start()
        return copy

    own_rows = pl.ds(pl.multiple_of(t * TOK, TOK), TOK)

    lx = local(x_hbm.at[0], xs)
    lh = local(h_hbm.at[0], hs)
    lg = local(g_hbm.at[0], gf.at[own_rows])
    lwo = local(wout_hbm.at[0], wout)
    lwi = local(win_hbm.at[0], win)

    barrier = pltpu.get_barrier_semaphore()
    for to in (core_dev, chip_dev, diag_dev, xp, xm, yp, ym, z_down, z_up):
        pl.semaphore_signal(barrier, inc=1, device_id=to, device_id_type=MESH)
    pl.semaphore_wait(barrier, 9)

    g_chip = remote(g_hbm.at[0], gf.at[own_rows], chip_dev)
    slot = plan_ref[0]
    lx.wait()
    halo[0] = xs[slot, TOK - 16 :, :]
    halo[1] = xs[slot, :16, :]
    h_next = remote(halo.at[0], halo.at[2], seq_next)
    h_prev = remote(halo.at[1], halo.at[3], seq_prev)
    g_core = remote(g_hbm.at[0], gf.at[own_rows], core_dev)

    def widen(i, carry):
        rows = pl.ds(pl.multiple_of(i * 16, 16), 16)
        xw[pl.ds(pl.multiple_of(16 + i * 16, 16), 16), :] = xs[slot, rows, :].astype(f32)
        return carry

    lax.fori_loop(0, TOK // 16, widen, 0)

    lh.wait()

    def gelu_rows(i, carry):
        rows = pl.ds(pl.multiple_of(i * 16, 16), 16)
        hv = hs[slot, rows, :].astype(f32)
        square = hv * hv
        tangent = jnp.tanh(root_coef * hv * (1.0 + gelu_coef * square))
        half = 0.5 + 0.5 * tangent
        value = hv * half
        active[rows, :] = value.astype(bf16)
        slope[rows, :] = half + value * (1.0 - tangent) * (
            root_coef + (3.0 * gelu_coef * root_coef) * square
        )
        return carry

    lax.fori_loop(0, SEQ // 16, gelu_rows, 0)

    h_next.wait_recv()
    h_prev.wait_recv()
    xw[0:16, :] = jnp.where(t > 0, halo[2].astype(f32), 0.0)
    xw[16 + TOK : 32 + TOK, :] = jnp.where(t < 3, halo[3].astype(f32), 0.0)

    def norm_rows(first, count):
        near = xw[pl.ds(first, count + 16), :]
        out = cb_ref[...] + cw_ref[0:1, :] * near[5 : 5 + count]
        for k in range(1, KER):
            out = out + cw_ref[k : k + 1, :] * near[5 + k : 5 + k + count]
        center = out - jnp.mean(out, -1, keepdims=True)
        istd = lax.rsqrt(jnp.mean(center * center, -1, keepdims=True) + norm_eps)
        return center * istd, istd

    def own_norm(i, carry):
        rows = pl.ds(pl.multiple_of(i * 16, 16), 16)
        value, istd = norm_rows(pl.multiple_of(16 * i + 8, 8), 16)
        normed[rows, :] = value
        inv[rows, :] = jnp.broadcast_to(istd, (16, 128))
        sf[pl.ds(pl.multiple_of(t * TOK + i * 16, 16), 16), :] = (
            value * gain_ref[...] + shift_ref[...]
        ).astype(bf16)
        return carry

    lax.fori_loop(0, TOK // 16, own_norm, 0)
    s_chip = remote(sf.at[own_rows], sf.at[own_rows], chip_dev)
    s_core = remote(sf.at[own_rows], sf.at[own_rows], core_dev)
    for first, row in ((0, TOK), (TOK + 8, TOK + 8)):
        value, istd = norm_rows(first, 8)
        normed[row : row + 8, :] = value
        inv[row : row + 8, :] = jnp.broadcast_to(istd, (8, 128))

    def hidden_grads(half):
        base = pl.multiple_of(half * 256, 256)
        for j in range(2):
            cols = pl.ds(j * CH, CH)
            d = dot_nt(gf[pl.ds(base, 256), :], wout[j * CH : (j + 1) * CH, :])
            d = d * slope[pl.ds(base, 256), cols]
            bias[:, cols] += jnp.sum(d, 0, keepdims=True)
            dh[pl.ds(base, 256), cols] = d.astype(bf16)

    def part_scaled(half):
        base = pl.multiple_of(half * 256, 256)

        def block(j, carry):
            cols = pl.ds(pl.multiple_of(j * CH, CH), CH)
            dpart[pl.ds(pl.multiple_of(base + 8, 8), 256), cols] = dot_nt(
                dh[pl.ds(base, 256), :], win[cols, :]
            )
            return carry

        lax.fori_loop(0, D // CH, block, 0)

    bias[...] = jnp.zeros_like(bias)
    dpart[0:8, :] = jnp.zeros((8, D), f32)
    dpart[SEQ + 8 : SEQ + 16, :] = jnp.zeros((8, D), f32)
    lwo.wait()
    lg.wait()
    g_core.wait_recv()
    hidden_grads(ylo)
    lwi.wait()
    part_scaled(ylo)

    g_chip.wait_recv()
    chip_rows = pl.ds(pl.multiple_of(((t + 2) % 4) * TOK, TOK), TOK)
    g_pass = remote(gf.at[chip_rows], gf.at[chip_rows], core_dev)
    g_pass.wait_recv()

    def weight_part(c, src, hidden):
        cols = pl.ds((c % 2) * CH, CH)

        def block(k, carry):
            target = pl.multiple_of(((xi + k) % 4) * XB, XB)
            part[c, k] = dot_tn(src[:, pl.ds(target, XB)], hidden[:, cols]).astype(bf16)
            return carry

        lax.fori_loop(0, 4, block, 0)

    def ring_first(own, two, last, half, plus, minus):
        far_a = remote(own.at[2, pl.ds(0, half)], two.at[0], plus)
        far_b = remote(own.at[2, pl.ds(half, half)], two.at[1], minus)
        near_b = remote(own.at[1, pl.ds(half, half)], last.at[0, pl.ds(half, half)], plus)
        near_a = remote(own.at[3, pl.ds(0, half)], last.at[1, pl.ds(0, half)], minus)
        return far_a, far_b, near_a, near_b

    def ring_second(copies, own, two, last, half, plus, minus):
        far_a, far_b, near_a, near_b = copies
        far_a.wait_recv()

        def add_a(i, carry):
            rows = pl.ds(pl.multiple_of(i * 48, 16), 48)
            own[1, rows, :] = (own[1, rows, :].astype(f32) + two[0, rows, :].astype(f32)).astype(bf16)
            return carry

        lax.fori_loop(0, half // 48, add_a, 0)
        sum_a = remote(own.at[1, pl.ds(0, half)], last.at[0, pl.ds(0, half)], plus)
        far_b.wait_recv()

        def add_b(i, carry):
            rows = pl.ds(pl.multiple_of(half + i * 48, 16), 48)
            here = pl.ds(pl.multiple_of(i * 48, 16), 48)
            own[3, rows, :] = (own[3, rows, :].astype(f32) + two[1, here, :].astype(f32)).astype(bf16)
            return carry

        lax.fori_loop(0, half // 48, add_b, 0)
        sum_b = remote(own.at[3, pl.ds(half, half)], last.at[1, pl.ds(half, half)], minus)
        return near_a, near_b, sum_a, sum_b

    x_copies, y_copies = {}, {}

    def x_first(c):
        x_copies[c] = ring_first(part.at[c], xr2.at[c], xrx.at[c], XB // 2, xp, xm)

    def x_second(c):
        x_copies[c] = ring_second(x_copies[c], part.at[c], xr2.at[c], xrx.at[c], XB // 2, xp, xm)

    def x_third(c):
        for copy in x_copies[c]:
            copy.wait_recv()

        def block(k, carry):
            for piece in range(2):
                rows = pl.ds(pl.multiple_of(((yi + k) % 4) * YB + piece * 48, 16), 48)
                q[c, k, pl.ds(piece * 48, 48), :] = (
                    part[c, 0, rows, :].astype(f32)
                    + xrx[c, 0, rows, :].astype(f32)
                    + xrx[c, 1, rows, :].astype(f32)
                ).astype(bf16)
            return carry

        lax.fori_loop(0, 4, block, 0)

    def y_first(c):
        y_copies[c] = ring_first(q.at[c], yr2.at[c], yrx.at[c], YB // 2, yp, ym)

    def y_second(c):
        y_copies[c] = ring_second(y_copies[c], q.at[c], yr2.at[c], yrx.at[c], YB // 2, yp, ym)

    def y_third(c):
        for copy in y_copies[c]:
            copy.wait_recv()
        out = gwo_out if c < 2 else gwi_out
        for piece in range(2):
            rows = pl.ds(piece * 48, 48)
            out[rows, pl.ds((c % 2) * CH, CH)] = (
                q[c, 0, rows, :].astype(f32)
                + yrx[c, 0, rows, :].astype(f32)
                + yrx[c, 1, rows, :].astype(f32)
            )

    weight_part(0, gf, active)
    x_first(0)

    hidden_grads(1 - ylo)
    part_scaled(1 - ylo)

    def target_rows(tt, i):
        return dpart[pl.ds(pl.multiple_of(8 + tt * TOK + i * 16, 8), 16), :]

    def target_rim(tt, after):
        return dpart[pl.ds(pl.multiple_of(tt * TOK + after * (TOK + 8), 8), 8), :]

    core_far = (1 - ylo) * 2 + 1 - core
    core_near = ylo * 2 + 1 - core
    core_sums = []
    for n, tt in enumerate((core_far, core_near)):

        def fill(i, carry, n=n, tt=tt):
            s1[n, pl.ds(pl.multiple_of(i * 16, 16), 16), :] = target_rows(tt, i).astype(bf16)
            return carry

        lax.fori_loop(0, TOK // 16, fill, 0)
        s1[n, TOK:, :] = jnp.concatenate([target_rim(tt, 0), target_rim(tt, 1)], 0).astype(bf16)
        core_sums.append(remote(s1.at[n], r1.at[n], core_dev))

    weight_part(1, gf, active)
    x_first(1)

    core_sums[0].wait_recv()
    chip_t = (t + 2) % 4

    def add_far(i, carry):
        rows = pl.ds(pl.multiple_of(i * 16, 16), 16)
        s2[rows, :] = (target_rows(chip_t, i) + r1[0, rows, :].astype(f32)).astype(bf16)
        return carry

    lax.fori_loop(0, TOK // 16, add_far, 0)
    s2[TOK:, :] = (
        jnp.concatenate([target_rim(chip_t, 0), target_rim(chip_t, 1)], 0) + r1[0, TOK:, :].astype(f32)
    ).astype(bf16)
    far_sum = remote(s2, r2t, chip_dev)

    x_second(0)

    s_chip.wait_recv()
    s_pass = remote(sf.at[chip_rows], sf.at[chip_rows], core_dev)
    s_core.wait_recv()
    s_pass.wait_recv()
    weight_part(2, sf, dh)
    x_first(2)
    x_second(1)
    weight_part(3, sf, dh)
    x_third(0)
    y_first(0)

    core_sums[1].wait_recv()
    far_sum.wait_recv()
    accs[...] = jnp.zeros_like(accs)

    def norm_back(ds, rows, count):
        nv = normed[rows, :]
        dn = ds * gain_ref[...]
        mean_d = jnp.mean(dn, -1, keepdims=True)
        mean_p = jnp.mean(dn * nv, -1, keepdims=True)
        return nv, inv[rows, 0:1] * (dn - mean_d - nv * mean_p)

    def own_back(i, carry):
        rows = pl.ds(pl.multiple_of(i * 16, 16), 16)
        ds = target_rows(t, i) + r1[1, rows, :].astype(f32) + r2t[rows, :].astype(f32)
        nv, dm = norm_back(ds, rows, 16)
        dmix[pl.ds(pl.multiple_of(8 + i * 16, 8), 16), :] = dm
        dsn = ds * nv
        accs[0] += dsn[0:8] + dsn[8:16]
        accs[1] += ds[0:8] + ds[8:16]
        return carry

    lax.fori_loop(0, TOK // 16, own_back, 0)
    rim = pl.ds(TOK, 16)
    rim_ds = (
        jnp.concatenate([target_rim(t, 0), target_rim(t, 1)], 0)
        + r1[1, TOK:, :].astype(f32)
        + r2t[TOK:, :].astype(f32)
    )
    _, rim_dm = norm_back(rim_ds, rim, 16)
    dmix[0:8, :] = rim_dm[0:8]
    dmix[TOK + 8 : TOK + 16, :] = rim_dm[8:16]


    def input_rows(i, carry):
        near = dmix[pl.ds(pl.multiple_of(16 * i, 16), 32), :]
        d = cw_ref[0:1, :] * near[11:27]
        for k in range(1, KER):
            d = d + cw_ref[k : k + 1, :] * near[11 - k : 27 - k]
        gv = gf[pl.ds(pl.multiple_of(t * TOK + i * 16, 16), 16), :].astype(f32)
        gx[pl.ds(pl.multiple_of(i * 16, 16), 16), :] = jnp.where(pz > 0, gv + d, 0.0).astype(bf16)
        return carry

    z_copies = []
    for piece in range(2):
        lax.fori_loop(piece * 4, piece * 4 + 4, input_rows, 0)
        rows = pl.ds(piece * 64, 64)
        z_copies.append(remote(gx.at[rows], gin_out.at[0, rows], z_down))

    x_first(3)

    sm[...] = jnp.zeros_like(sm)

    def tap_sums(j, carry):
        cols = pl.ds(pl.multiple_of(j * 256, 256), 256)

        def rows_step(i, totals):
            dm = dmix[pl.ds(pl.multiple_of(8 + 8 * i, 8), 8), cols]
            near = xw[pl.ds(pl.multiple_of(8 + 8 * i, 8), 24), cols]
            out = [totals[k] + dm * near[5 + k : 13 + k] for k in range(KER)]
            out.append(totals[KER] + dm)
            return tuple(out)

        totals = lax.fori_loop(
            0, TOK // 8, rows_step, tuple(jnp.zeros((8, 256), f32) for _ in range(KER + 1))
        )
        for k in range(KER + 1):
            sm[k : k + 1, cols] = jnp.sum(totals[k], 0, keepdims=True)

        def g_step(i, total):
            gv = gf[pl.ds(pl.multiple_of(t * TOK + i * 16, 16), 16), cols].astype(f32)
            return total + gv[0:8] + gv[8:16]

        total = lax.fori_loop(0, TOK // 16, g_step, jnp.zeros((8, 256), f32))
        sm[10:11, cols] = jnp.sum(total, 0, keepdims=True)
        sm[8:9, cols] = jnp.sum(accs[0, :, cols], 0, keepdims=True)
        sm[9:10, cols] = jnp.sum(accs[1, :, cols], 0, keepdims=True)
        return carry

    lax.fori_loop(0, D // 256, tap_sums, 0)
    zero_row = jnp.zeros((1, HID), f32)
    for s in range(4):
        sm[11 + s // 2 : 12 + s // 2, (s % 2) * HID : (s % 2 + 1) * HID] = jnp.where(
            t == s, bias[...], zero_row
        )
    a_core = remote(sm, arc, core_dev)

    x_second(2)

    a_core.wait_recv()
    my8 = pl.ds(pl.multiple_of(core * 8, 8), 8)
    ar[0] = sm[my8, :] + arc[my8, :]
    partners = (chip_dev, x_a, x_b, y_a, y_b)
    a_copy = remote(ar.at[0], arr.at[0], partners[0])

    def a_step(n):
        a_copy.wait_recv()
        ar[n] = ar[n - 1] + arr[n - 1]
        if n < len(partners):
            return remote(ar.at[n], arr.at[n], partners[n])
        return None

    x_third(1)
    y_first(1)
    a_copy = a_step(1)
    y_second(0)
    y_third(0)
    a_copy = a_step(2)
    x_second(3)
    a_copy = a_step(3)
    x_third(2)
    y_first(2)
    a_copy = a_step(4)
    y_second(1)
    y_third(1)
    a_step(5)
    small_out[my8, :] = ar[5]
    a_back = remote(ar.at[5], small_out.at[my8], core_dev)
    y_second(2)
    x_third(3)
    y_first(3)
    y_third(2)
    y_second(3)
    y_third(3)
    a_back.wait_recv()
    for copy in z_copies:
        copy.wait_recv()
    for copy in sent:
        copy.wait_send()


def per_device(x_stash, h_stash, cotangent, plan, conv_w, conv_b, norm_gain, shift_b, w_in, w_out):
    anyspace = pl.BlockSpec(memory_space=pl.ANY)
    vmem = pl.BlockSpec(memory_space=pltpu.VMEM)
    smem = pl.BlockSpec(memory_space=pltpu.SMEM)
    gin, gwi, gwo, small = pl.pallas_call(
        kernel,
        out_shape=(
            jax.ShapeDtypeStruct((1, TOK, D), bf16),
            jax.ShapeDtypeStruct((YB, HID), f32),
            jax.ShapeDtypeStruct((YB, HID), f32),
            jax.ShapeDtypeStruct((16, D), f32),
        ),
        in_specs=[anyspace, anyspace, anyspace, smem, vmem, vmem, vmem, vmem, anyspace, anyspace],
        out_specs=(anyspace, vmem, vmem, vmem),
        scratch_shapes=[
            pltpu.VMEM((2, TOK, D), bf16),
            pltpu.VMEM((2, SEQ, HID), bf16),
            pltpu.VMEM((SEQ, D), bf16),
            pltpu.VMEM((SEQ, D), bf16),
            pltpu.VMEM((D, HID), bf16),
            pltpu.VMEM((HID, D), bf16),
            pltpu.VMEM((4, 16, D), bf16),
            pltpu.VMEM((TOK + 32, D), f32),
            pltpu.VMEM((WIDE, D), f32),
            pltpu.VMEM((WIDE, 128), f32),
            pltpu.VMEM((SEQ, HID), bf16),
            pltpu.VMEM((SEQ, HID), f32),
            pltpu.VMEM((SEQ, HID), bf16),
            pltpu.VMEM((SEQ + 16, D), f32),
            pltpu.VMEM((2, WIDE, D), bf16),
            pltpu.VMEM((2, WIDE, D), bf16),
            pltpu.VMEM((WIDE, D), bf16),
            pltpu.VMEM((WIDE, D), bf16),
            pltpu.VMEM((4, 4, XB, CH), bf16),
            pltpu.VMEM((4, 2, XB // 2, CH), bf16),
            pltpu.VMEM((4, 2, XB, CH), bf16),
            pltpu.VMEM((4, 4, YB, CH), bf16),
            pltpu.VMEM((4, 2, YB // 2, CH), bf16),
            pltpu.VMEM((4, 2, YB, CH), bf16),
            pltpu.VMEM((WIDE, D), f32),
            pltpu.VMEM((TOK, D), bf16),
            pltpu.VMEM((2, 8, D), f32),
            pltpu.VMEM((16, D), f32),
            pltpu.VMEM((16, D), f32),
            pltpu.VMEM((6, 8, D), f32),
            pltpu.VMEM((5, 8, D), f32),
            pltpu.VMEM((1, HID), f32),
            pltpu.SemaphoreType.DMA((N_COPIES,)),
            pltpu.SemaphoreType.DMA((N_COPIES,)),
            pltpu.SemaphoreType.DMA((N_LOCAL,)),
        ],
        compiler_params=pltpu.CompilerParams(
            collective_id=0, has_side_effects=True, vmem_limit_bytes=56 * 1024 * 1024
        ),
    )(
        x_stash, h_stash, cotangent, plan, conv_w[0], conv_b, norm_gain, shift_b, w_in, w_out
    )
    return (
        gin,
        gwi[None],
        gwo.T[None],
        small[None, 0:8],
        small[None, 8:11],
        small[11:13].reshape(1, 2 * D),
    )


def solution(mesh):
    return jax.shard_map(
        per_device,
        mesh=mesh,
        in_specs=(
            P("pipe", None, ("dp", "tensor"), None),
            P("pipe", None, "dp", "tensor"),
            P("pipe", ("dp", "tensor"), None),
            P("pipe"),
            P("pipe", None, None),
            P("pipe", None),
            P("pipe", None),
            P("pipe", None),
            P("pipe", None, "tensor"),
            P("pipe", "tensor", None),
        ),
        out_specs=(
            P("pipe", ("dp", "tensor"), None),
            P("pipe", "dp", "tensor"),
            P("pipe", "tensor", "dp"),
            P("pipe", None, None),
            P("pipe", None, None),
            P("pipe", None),
        ),
        check_vma=False,
    )
```

time: 454 us -> 117 us (0.26)
  the two profiles are of different devices: /device:TPU:1 before, /device:TPU:8 now
where the time goes in v1:
time: 117 us; the launch traced here: 116 us
  Pallas kernels  104 us (89%)
  local copies, waits for them, and re-layouts  10.8 us (9%)
  between operations  1.29 us (1%)
    pallas_call x1, Pallas kernels, per_device(): pl.pallas_call(kernel, out_shape=(jax.ShapeDtypeStruct((1, TOK, D), bf16)...  104 us
    unnamed x7, local copies, waits for them, and re-layouts  8.6 us

profile of v1, /device:TPU:8, one launch (start us, length us, event | category | flops | bytes accessed | tf_op | source)
XLA Modules:
  0.0 116.1 jit_solution(16001787231109255777)
XLA Ops:
  0.6 1.4 %copy.20 = f32[1,7,1536]{2,1,0:T(8,128)} copy(f32[1,7,1536]{2,0,1:T(1,128)} %param.14) | data formatting | bytes 86016
  2.7 104.0 %shard_map.145 = (bf16[1,128,1536]{2,1,0:T(8,128)(2,1)}, f32[96,768]{1,0:T(8,128)}, f32[96,768]{1,0:T(8,128)}, f32[16,1536]{1,0:T(8,128)}) custom-call(bf16[1,2,128,1536]{3,2,1,0:T(8,128)(2,1)} %x_hbm.1, bf16[1,2,512,768]{3,2,1,0:T(8,128)(2,1)} %h_hbm.1, bf16[1,128,1536]{2,1,0:T(8,128)(2,1)} %g_hbm.1, s32[1]{0:T(128)S(6)} %copy.24.plan_ref, ...), custom_call_target="tpu_custom_call" | custom-call | tf_op jit(solution)/shard_map/pallas_call | solution.py:480
  106.7 1.4 %slice_bitcast_fusion = f32[1,8,1536]{2,1,0:T(8,128)} fusion(f32[16,1536]{1,0:T(8,128)} %get-tuple-element.13), kind=kLoop, calls=%fused_computation.1 | loop fusion | bytes 98304 | tf_op jit(solution)/shard_map/broadcast_in_dim | solution.py:537
  108.1 0.8 slice_bitcast_fusion.1
  108.9 0.6 copy.16
  109.6 0.8 slice_bitcast_fusion.2
  110.4 0.6 copy.18
  111.0 1.8 %copy.25 = bf16[1,128,1536]{2,1,0:T(8,128)(2,1)} copy(bf16[1,128,1536]{2,1,0:T(8,128)(2,1)} %get-tuple-element.26) | data formatting | bytes 786432
  112.8 1.7 %copy.26 = f32[1,96,768]{2,1,0:T(8,128)} copy(f32[1,96,768]{2,1,0:T(8,128)} %bitcast.16) | data formatting | bytes 589824
  114.4 1.7 %copy.27 = f32[1,768,96]{1,2,0:T(8,128)} copy(f32[1,768,96]{1,2,0:T(8,128)} %bitcast.15) | data formatting | bytes 589824

commit v2 on v1

--- a/solution.py
+++ b/solution.py
@@ -24,7 +24,7 @@
 XB = D // 4
 YB = XB // 4
 WIDE = TOK + 16
-N_COPIES = 96
+N_COPIES = 112
 N_LOCAL = 16
 
 
@@ -105,14 +105,30 @@
         pl.semaphore_signal(barrier, inc=1, device_id=to, device_id_type=MESH)
     pl.semaphore_wait(barrier, 9)
 
-    g_chip = remote(g_hbm.at[0], gf.at[own_rows], chip_dev)
+    def block_cols(k):
+        return pl.ds(pl.multiple_of(((xi + k) % 4) * XB, XB), XB)
+
+    order = (2, 1, 3, 0)
+    chip_rows = pl.ds(pl.multiple_of(((t + 2) % 4) * TOK, TOK), TOK)
+
+    def pass_on(copies, full, k):
+        copies[k].wait_recv()
+        chip_block = full.at[chip_rows, block_cols(k)]
+        return remote(chip_block, chip_block, core_dev)
+
+    def send_g(k, to):
+        return remote(g_hbm.at[0, :, block_cols(k)], gf.at[own_rows, block_cols(k)], to)
+
+    g_chip = {2: send_g(2, chip_dev)}
     slot = plan_ref[0]
     lx.wait()
     halo[0] = xs[slot, TOK - 16 :, :]
     halo[1] = xs[slot, :16, :]
     h_next = remote(halo.at[0], halo.at[2], seq_next)
     h_prev = remote(halo.at[1], halo.at[3], seq_prev)
-    g_core = remote(g_hbm.at[0], gf.at[own_rows], core_dev)
+    for k in order[1:]:
+        g_chip[k] = send_g(k, chip_dev)
+    g_core = {k: send_g(k, core_dev) for k in order}
 
     def widen(i, carry):
         rows = pl.ds(pl.multiple_of(i * 16, 16), 16)
@@ -145,9 +161,9 @@
 
     def norm_rows(first, count):
         near = xw[pl.ds(first, count + 16), :]
-        out = cb_ref[...] + cw_ref[0:1, :] * near[5 : 5 + count]
+        out = cb_ref[...] + cw_ref[0] * near[5 : 5 + count]
         for k in range(1, KER):
-            out = out + cw_ref[k : k + 1, :] * near[5 + k : 5 + k + count]
+            out = out + cw_ref[k] * near[5 + k : 5 + k + count]
         center = out - jnp.mean(out, -1, keepdims=True)
         istd = lax.rsqrt(jnp.mean(center * center, -1, keepdims=True) + norm_eps)
         return center * istd, istd
@@ -162,14 +178,16 @@
         ).astype(bf16)
         return carry
 
-    lax.fori_loop(0, TOK // 16, own_norm, 0)
-    s_chip = remote(sf.at[own_rows], sf.at[own_rows], chip_dev)
-    s_core = remote(sf.at[own_rows], sf.at[own_rows], core_dev)
-    for first, row in ((0, TOK), (TOK + 8, TOK + 8)):
-        value, istd = norm_rows(first, 8)
-        normed[row : row + 8, :] = value
-        inv[row : row + 8, :] = jnp.broadcast_to(istd, (8, 128))
-
+    lax.fori_loop(0, TOK // 32, own_norm, 0)
+    g_pass = {2: pass_on(g_chip, gf, 2)}
+    lax.fori_loop(TOK // 32, TOK // 16, own_norm, 0)
+
+    def send_s(k, to):
+        own_block = sf.at[own_rows, block_cols(k)]
+        return remote(own_block, own_block, to)
+
+    s_chip = {k: send_s(k, chip_dev) for k in order}
+    s_core = {k: send_s(k, core_dev) for k in order}
     def hidden_grads(half):
         base = pl.multiple_of(half * 256, 256)
         for j in range(2):
@@ -191,37 +209,20 @@
 
         lax.fori_loop(0, D // CH, block, 0)
 
-    bias[...] = jnp.zeros_like(bias)
-    dpart[0:8, :] = jnp.zeros((8, D), f32)
-    dpart[SEQ + 8 : SEQ + 16, :] = jnp.zeros((8, D), f32)
-    lwo.wait()
-    lg.wait()
-    g_core.wait_recv()
-    hidden_grads(ylo)
-    lwi.wait()
-    part_scaled(ylo)
-
-    g_chip.wait_recv()
-    chip_rows = pl.ds(pl.multiple_of(((t + 2) % 4) * TOK, TOK), TOK)
-    g_pass = remote(gf.at[chip_rows], gf.at[chip_rows], core_dev)
-    g_pass.wait_recv()
-
-    def weight_part(c, src, hidden):
-        cols = pl.ds((c % 2) * CH, CH)
-
-        def block(k, carry):
-            target = pl.multiple_of(((xi + k) % 4) * XB, XB)
-            part[c, k] = dot_tn(src[:, pl.ds(target, XB)], hidden[:, cols]).astype(bf16)
-            return carry
-
-        lax.fori_loop(0, 4, block, 0)
-
-    def ring_first(own, two, last, half, plus, minus):
+    def weight_part(c, k, src, hidden):
+        block = dot_tn(src[:, block_cols(k)], hidden[...]).astype(bf16)
+        part[c, k] = block[:, :CH]
+        part[c + 1, k] = block[:, CH:]
+
+    def ring_far(own, two, half, plus, minus):
         far_a = remote(own.at[2, pl.ds(0, half)], two.at[0], plus)
         far_b = remote(own.at[2, pl.ds(half, half)], two.at[1], minus)
+        return far_a, far_b
+
+    def ring_near(own, last, half, plus, minus):
         near_b = remote(own.at[1, pl.ds(half, half)], last.at[0, pl.ds(half, half)], plus)
         near_a = remote(own.at[3, pl.ds(0, half)], last.at[1, pl.ds(0, half)], minus)
-        return far_a, far_b, near_a, near_b
+        return near_a, near_b
 
     def ring_second(copies, own, two, last, half, plus, minus):
         far_a, far_b, near_a, near_b = copies
@@ -248,8 +249,11 @@
 
     x_copies, y_copies = {}, {}
 
-    def x_first(c):
-        x_copies[c] = ring_first(part.at[c], xr2.at[c], xrx.at[c], XB // 2, xp, xm)
+    def x_far(c):
+        x_copies[c] = ring_far(part.at[c], xr2.at[c], XB // 2, xp, xm)
+
+    def x_near(c):
+        x_copies[c] += ring_near(part.at[c], xrx.at[c], XB // 2, xp, xm)
 
     def x_second(c):
         x_copies[c] = ring_second(x_copies[c], part.at[c], xr2.at[c], xrx.at[c], XB // 2, xp, xm)
@@ -271,7 +275,8 @@
         lax.fori_loop(0, 4, block, 0)
 
     def y_first(c):
-        y_copies[c] = ring_first(q.at[c], yr2.at[c], yrx.at[c], YB // 2, yp, ym)
+        y_copies[c] = ring_far(q.at[c], yr2.at[c], YB // 2, yp, ym)
+        y_copies[c] += ring_near(q.at[c], yrx.at[c], YB // 2, yp, ym)
 
     def y_second(c):
         y_copies[c] = ring_second(y_copies[c], q.at[c], yr2.at[c], yrx.at[c], YB // 2, yp, ym)
@@ -288,9 +293,37 @@
                 + yrx[c, 1, rows, :].astype(f32)
             )
 
-    weight_part(0, gf, active)
-    x_first(0)
-
+    lg.wait()
+    for k in order:
+        g_core[k].wait_recv()
+    g_pass[2].wait_recv()
+    weight_part(0, 2, gf, active)
+    x_far(0)
+    x_far(1)
+
+    for first, row in ((0, TOK), (TOK + 8, TOK + 8)):
+        value, istd = norm_rows(first, 8)
+        normed[row : row + 8, :] = value
+        inv[row : row + 8, :] = jnp.broadcast_to(istd, (8, 128))
+
+    bias[...] = jnp.zeros_like(bias)
+    dpart[0:8, :] = jnp.zeros((8, D), f32)
+    dpart[SEQ + 8 : SEQ + 16, :] = jnp.zeros((8, D), f32)
+    lwo.wait()
+    hidden_grads(ylo)
+    g_pass[1] = pass_on(g_chip, gf, 1)
+    lwi.wait()
+    part_scaled(ylo)
+
+    g_pass[3] = pass_on(g_chip, gf, 3)
+    g_pass[1].wait_recv()
+    weight_part(0, 1, gf, active)
+    g_pass[0] = pass_on(g_chip, gf, 0)
+    g_pass[3].wait_recv()
+    weight_part(0, 3, gf, active)
+    x_near(0)
+    x_near(1)
+    g_pass[0].wait_recv()
     hidden_grads(1 - ylo)
     part_scaled(1 - ylo)
 
@@ -313,8 +346,8 @@
         s1[n, TOK:, :] = jnp.concatenate([target_rim(tt, 0), target_rim(tt, 1)], 0).astype(bf16)
         core_sums.append(remote(s1.at[n], r1.at[n], core_dev))
 
-    weight_part(1, gf, active)
-    x_first(1)
+    weight_part(0, 0, gf, active)
+    x_second(0)
 
     core_sums[0].wait_recv()
     chip_t = (t + 2) % 4
@@ -330,18 +363,28 @@
     ).astype(bf16)
     far_sum = remote(s2, r2t, chip_dev)
 
-    x_second(0)
-
-    s_chip.wait_recv()
-    s_pass = remote(sf.at[chip_rows], sf.at[chip_rows], core_dev)
-    s_core.wait_recv()
-    s_pass.wait_recv()
-    weight_part(2, sf, dh)
-    x_first(2)
     x_second(1)
-    weight_part(3, sf, dh)
+    s_pass = {2: pass_on(s_chip, sf, 2)}
+    for k in order:
+        s_core[k].wait_recv()
+    s_pass[2].wait_recv()
+    weight_part(2, 2, sf, dh)
+    x_far(2)
+    x_far(3)
+    for k in order[1:]:
+        s_pass[k] = pass_on(s_chip, sf, k)
+    s_pass[1].wait_recv()
+    weight_part(2, 1, sf, dh)
+    s_pass[3].wait_recv()
+    weight_part(2, 3, sf, dh)
+    x_near(2)
+    x_near(3)
+    s_pass[0].wait_recv()
+    weight_part(2, 0, sf, dh)
     x_third(0)
     y_first(0)
+    x_third(1)
+    y_first(1)
 
     core_sums[1].wait_recv()
     far_sum.wait_recv()
@@ -378,9 +421,9 @@
 
     def input_rows(i, carry):
         near = dmix[pl.ds(pl.multiple_of(16 * i, 16), 32), :]
-        d = cw_ref[0:1, :] * near[11:27]
+        d = cw_ref[0] * near[11:27]
         for k in range(1, KER):
-            d = d + cw_ref[k : k + 1, :] * near[11 - k : 27 - k]
+            d = d + cw_ref[k] * near[11 - k : 27 - k]
         gv = gf[pl.ds(pl.multiple_of(t * TOK + i * 16, 16), 16), :].astype(f32)
         gx[pl.ds(pl.multiple_of(i * 16, 16), 16), :] = jnp.where(pz > 0, gv + d, 0.0).astype(bf16)
         return carry
@@ -390,8 +433,6 @@
         lax.fori_loop(piece * 4, piece * 4 + 4, input_rows, 0)
         rows = pl.ds(piece * 64, 64)
         z_copies.append(remote(gx.at[rows], gin_out.at[0, rows], z_down))
-
-    x_first(3)
 
     sm[...] = jnp.zeros_like(sm)
 
@@ -429,8 +470,8 @@
         )
     a_core = remote(sm, arc, core_dev)
 
-    x_second(2)
-
+    y_second(0)
+    y_second(1)
     a_core.wait_recv()
     my8 = pl.ds(pl.multiple_of(core * 8, 8), 8)
     ar[0] = sm[my8, :] + arc[my8, :]
@@ -444,27 +485,24 @@
             return remote(ar.at[n], arr.at[n], partners[n])
         return None
 
-    x_third(1)
-    y_first(1)
+    x_second(2)
+    x_second(3)
     a_copy = a_step(1)
-    y_second(0)
     y_third(0)
+    y_third(1)
     a_copy = a_step(2)
-    x_second(3)
     a_copy = a_step(3)
     x_third(2)
     y_first(2)
     a_copy = a_step(4)
-    y_second(1)
-    y_third(1)
+    x_third(3)
+    y_first(3)
     a_step(5)
     small_out[my8, :] = ar[5]
     a_back = remote(ar.at[5], small_out.at[my8], core_dev)
     y_second(2)
-    x_third(3)
-    y_first(3)
+    y_second(3)
     y_third(2)
-    y_second(3)
     y_third(3)
     a_back.wait_recv()
     for copy in z_copies:
@@ -473,11 +511,22 @@
         copy.wait_send()
 
 
+def deliver(gin, gwi, gwo, small, gin_out, gwi_out, gwo_out, conv_out, affine_out, bias_out):
+    gin_out[...] = gin[...]
+    gwi_out[...] = gwi[...]
+    gwo_out[...] = gwo[...]
+    conv_out[...] = small[0:8, :]
+    for i in range(3):
+        affine_out[i] = small[8 + i : 9 + i, :]
+    for i in range(2):
+        bias_out[:, i * D : (i + 1) * D] = small[11 + i : 12 + i, :]
+
+
 def per_device(x_stash, h_stash, cotangent, plan, conv_w, conv_b, norm_gain, shift_b, w_in, w_out):
     anyspace = pl.BlockSpec(memory_space=pl.ANY)
     vmem = pl.BlockSpec(memory_space=pltpu.VMEM)
     smem = pl.BlockSpec(memory_space=pltpu.SMEM)
-    gin, gwi, gwo, small = pl.pallas_call(
+    results = pl.pallas_call(
         kernel,
         out_shape=(
             jax.ShapeDtypeStruct((1, TOK, D), bf16),
@@ -528,15 +577,28 @@
             collective_id=0, has_side_effects=True, vmem_limit_bytes=56 * 1024 * 1024
         ),
     )(
-        x_stash, h_stash, cotangent, plan, conv_w[0], conv_b, norm_gain, shift_b, w_in, w_out
+        x_stash, h_stash, cotangent, plan, jnp.swapaxes(conv_w, 0, 1), conv_b, norm_gain, shift_b, w_in, w_out
     )
+    gin, gwi, gwo, conv, affine, bias = pl.pallas_call(
+        deliver,
+        out_shape=(
+            jax.ShapeDtypeStruct((1, TOK, D), bf16),
+            jax.ShapeDtypeStruct((YB, HID), f32),
+            jax.ShapeDtypeStruct((YB, HID), f32),
+            jax.ShapeDtypeStruct((8, D), f32),
+            jax.ShapeDtypeStruct((3, 1, D), f32),
+            jax.ShapeDtypeStruct((1, 2 * D), f32),
+        ),
+        in_specs=[vmem] * 4,
+        out_specs=(vmem,) * 6,
+    )(*results)
     return (
         gin,
         gwi[None],
         gwo.T[None],
-        small[None, 0:8],
-        small[None, 8:11],
-        small[11:13].reshape(1, 2 * D),
+        conv[None],
+        jnp.swapaxes(affine, 0, 1),
+        bias,
     )
 
 

time: 117 us -> 93.3 us (0.80)
  Pallas kernels: 104 us -> 91.7 us
  local copies, waits for them, and re-layouts: 10.8 us -> 0 us
    pallas_call x1, Pallas kernels: 104 us -> 89.6 us  [per_device(): pl.pallas_call(kernel, out_shape=(jax.ShapeDtypeStruct((1, TOK, D), bf16)...]
    unnamed x7 -> x0, local copies, waits for them, and re-layouts: 8.6 us -> none
    broadcast_in_dim x2 -> x0, local copies, waits for them, and re-layouts: 2.22 us -> none  [the longest x1 1.42 us: per_device(): small[None, 0:8]]
    pallas_call x0 -> x1, Pallas kernels: none -> 2.17 us  [per_device(): pl.pallas_call(deliver, out_shape=(jax.ShapeDtypeStruct((1, TOK, D), bf16...]
where the time goes in v2:
time: 93.3 us; the launch traced here: 93 us
  Pallas kernels  91.7 us (98%)
  between operations  1.29 us (1%)
    pallas_call x1, Pallas kernels, per_device(): pl.pallas_call(kernel, out_shape=(jax.ShapeDtypeStruct((1, TOK, D), bf16)...  89.6 us
    pallas_call x1, Pallas kernels, per_device(): pl.pallas_call(deliver, out_shape=(jax.ShapeDtypeStruct((1, TOK, D), bf16...  2.17 us

profile of v2, /device:TPU:8, one launch (start us, length us, event | category | flops | bytes accessed | tf_op | source)
XLA Modules:
  0.0 93.0 jit_solution(15615313174300681884)
XLA Ops:
  1.3 89.6 %shard_map.145 = (bf16[1,128,1536]{2,1,0:T(8,128)(2,1)}, f32[96,768]{1,0:T(8,128)}, f32[96,768]{1,0:T(8,128)}, f32[16,1536]{1,0:T(8,128)}) custom-call(bf16[1,2,128,1536]{3,2,1,0:T(8,128)(2,1)} %x_hbm.1, bf16[1,2,512,768]{3,2,1,0:T(8,128)(2,1)} %h_hbm.1, bf16[1,128,1536]{2,1,0:T(8,128)(2,1)} %g_hbm.1, s32[1]{0:T(128)S(6)} %copy.16.plan_ref, ...), custom_call_target="tpu_custom_call" | custom-call | tf_op jit(solution)/shard_map/pallas_call | solution.py:529
  90.9 2.2 %shard_map.146 = (bf16[1,128,1536]{2,1,0:T(8,128)(2,1)}, f32[96,768]{1,0:T(8,128)}, f32[96,768]{1,0:T(8,128)}, f32[8,1536]{1,0:T(8,128)}, f32[3,1,1536]{2,1,0:T(1,128)}, /*index=5*/f32[1,3072]{1,0:T(1,128)}) custom-call(bf16[1,128,1536]{2,1,0:T(8,128)(2,1)} %get-tuple-element.16.gin, f32[96,768]{1,0:T(8,128)} %get-tuple-element.17.gwi, ...), custom_call_target="tpu_custom_call" | custom-call | tf_op jit(solution)/shard_map/pallas_call | solution.py:582

commit v3 on v2

--- a/solution.py
+++ b/solution.py
@@ -37,10 +37,10 @@
 
 
 def kernel(
-    x_hbm, h_hbm, g_hbm, plan_ref, cw_ref, cb_ref, gain_ref, shift_ref, win_hbm, wout_hbm,
-    gin_out, gwi_out, gwo_out, small_out,
+    x_hbm, h_hbm, g_hbm, plan_ref, cw_hbm, cb_hbm, gain_hbm, shift_hbm, win_hbm, wout_hbm,
+    gin_out, gwi_out, gwo_out, small_out, cw_ref, cb_ref, gain_ref, shift_ref,
     xs, hs, gf, sf, win, wout, halo, xw, normed, inv, active, slope, dh, dpart, s1, r1, s2, r2t,
-    part, xr2, xrx, q, yr2, yrx, dmix, gx, accs, sm, arc, ar, arr, bias, ssem, rsem, lsem,
+    part, xr2, xrx, q, yr2, yrx, dmix, gx, accs, sm, arc, ar, arr, arx, ary, arf, bias, ssem, rsem, lsem,
 ):
     dp = lax.axis_index("dp")
     pz = lax.axis_index("pipe")
@@ -62,10 +62,7 @@
     seq_next, seq_prev = dev(t_=(t + 1) % 4), dev(t_=(t + 3) % 4)
     xp, xm = dev(dp_=((xi + 1) % 4) * 4 + yi), dev(dp_=((xi + 3) % 4) * 4 + yi)
     yp, ym = dev(dp_=xi * 4 + (yi + 1) % 4), dev(dp_=xi * 4 + (yi + 3) % 4)
-    x_a = dev(dp_=(xi + 1 - 2 * (xi % 2)) * 4 + yi)
-    x_b = dev(dp_=(3 - xi) * 4 + yi)
-    y_a = dev(dp_=xi * 4 + yi + 1 - 2 * (yi % 2))
-    y_b = dev(dp_=xi * 4 + 3 - yi)
+    x2, y2 = dev(dp_=((xi + 2) % 4) * 4 + yi), dev(dp_=xi * 4 + (yi + 2) % 4)
     z_down = dev(pz_=(pz + npipe - 1) % npipe)
     z_up = dev(pz_=(pz + 1) % npipe)
 
@@ -94,16 +91,12 @@
 
     own_rows = pl.ds(pl.multiple_of(t * TOK, TOK), TOK)
 
+    barrier = pltpu.get_barrier_semaphore()
+    for to in (core_dev, chip_dev, diag_dev, xp, xm, x2, yp, ym, y2, z_down, z_up):
+        pl.semaphore_signal(barrier, inc=1, device_id=to, device_id_type=MESH)
     lx = local(x_hbm.at[0], xs)
     lh = local(h_hbm.at[0], hs)
-    lg = local(g_hbm.at[0], gf.at[own_rows])
-    lwo = local(wout_hbm.at[0], wout)
-    lwi = local(win_hbm.at[0], win)
-
-    barrier = pltpu.get_barrier_semaphore()
-    for to in (core_dev, chip_dev, diag_dev, xp, xm, yp, ym, z_down, z_up):
-        pl.semaphore_signal(barrier, inc=1, device_id=to, device_id_type=MESH)
-    pl.semaphore_wait(barrier, 9)
+    pl.semaphore_wait(barrier, 11)
 
     def block_cols(k):
         return pl.ds(pl.multiple_of(((xi + k) % 4) * XB, XB), XB)
@@ -129,6 +122,12 @@
     for k in order[1:]:
         g_chip[k] = send_g(k, chip_dev)
     g_core = {k: send_g(k, core_dev) for k in order}
+    small_loads = [
+        local(cw_hbm, cw_ref), local(cb_hbm, cb_ref), local(gain_hbm, gain_ref), local(shift_hbm, shift_ref)
+    ]
+    lg = local(g_hbm.at[0], gf.at[own_rows])
+    lwo = local(wout_hbm.at[0], wout)
+    lwi = local(win_hbm.at[0], win)
 
     def widen(i, carry):
         rows = pl.ds(pl.multiple_of(i * 16, 16), 16)
@@ -154,6 +153,8 @@
 
     lax.fori_loop(0, SEQ // 16, gelu_rows, 0)
 
+    for copy in small_loads:
+        copy.wait()
     h_next.wait_recv()
     h_prev.wait_recv()
     xw[0:16, :] = jnp.where(t > 0, halo[2].astype(f32), 0.0)
@@ -322,7 +323,6 @@
     g_pass[3].wait_recv()
     weight_part(0, 3, gf, active)
     x_near(0)
-    x_near(1)
     g_pass[0].wait_recv()
     hidden_grads(1 - ylo)
     part_scaled(1 - ylo)
@@ -348,6 +348,7 @@
 
     weight_part(0, 0, gf, active)
     x_second(0)
+    x_near(1)
 
     core_sums[0].wait_recv()
     chip_t = (t + 2) % 4
@@ -370,7 +371,6 @@
     s_pass[2].wait_recv()
     weight_part(2, 2, sf, dh)
     x_far(2)
-    x_far(3)
     for k in order[1:]:
         s_pass[k] = pass_on(s_chip, sf, k)
     s_pass[1].wait_recv()
@@ -378,13 +378,11 @@
     s_pass[3].wait_recv()
     weight_part(2, 3, sf, dh)
     x_near(2)
-    x_near(3)
+    x_far(3)
     s_pass[0].wait_recv()
     weight_part(2, 0, sf, dh)
     x_third(0)
     y_first(0)
-    x_third(1)
-    y_first(1)
 
     core_sums[1].wait_recv()
     far_sum.wait_recv()
@@ -470,37 +468,36 @@
         )
     a_core = remote(sm, arc, core_dev)
 
-    y_second(0)
-    y_second(1)
+    x_second(2)
+    x_near(3)
     a_core.wait_recv()
     my8 = pl.ds(pl.multiple_of(core * 8, 8), 8)
-    ar[0] = sm[my8, :] + arc[my8, :]
-    partners = (chip_dev, x_a, x_b, y_a, y_b)
-    a_copy = remote(ar.at[0], arr.at[0], partners[0])
-
-    def a_step(n):
-        a_copy.wait_recv()
-        ar[n] = ar[n - 1] + arr[n - 1]
-        if n < len(partners):
-            return remote(ar.at[n], arr.at[n], partners[n])
-        return None
-
-    x_second(2)
+    ar[...] = sm[my8, :] + arc[my8, :]
+    a_chip = remote(ar, arr, chip_dev)
+    x_third(1)
+    y_first(1)
+    y_second(0)
     x_second(3)
-    a_copy = a_step(1)
+    a_chip.wait_recv()
+    arx[xi] = ar[...] + arr[...]
+    a_x = [remote(arx.at[xi], arx.at[xi], to) for to in (xp, xm, x2)]
     y_third(0)
-    y_third(1)
-    a_copy = a_step(2)
-    a_copy = a_step(3)
+    y_second(1)
     x_third(2)
     y_first(2)
-    a_copy = a_step(4)
+    y_third(1)
+    for copy in a_x:
+        copy.wait_recv()
+    ary[yi] = (arx[0] + arx[1]) + (arx[2] + arx[3])
+    a_y = [remote(ary.at[yi], ary.at[yi], to) for to in (yp, ym, y2)]
     x_third(3)
     y_first(3)
-    a_step(5)
-    small_out[my8, :] = ar[5]
-    a_back = remote(ar.at[5], small_out.at[my8], core_dev)
     y_second(2)
+    for copy in a_y:
+        copy.wait_recv()
+    arf[...] = (ary[0] + ary[1]) + (ary[2] + ary[3])
+    small_out[my8, :] = arf[...]
+    a_back = remote(arf, small_out.at[my8], core_dev)
     y_second(3)
     y_third(2)
     y_third(3)
@@ -534,9 +531,13 @@
             jax.ShapeDtypeStruct((YB, HID), f32),
             jax.ShapeDtypeStruct((16, D), f32),
         ),
-        in_specs=[anyspace, anyspace, anyspace, smem, vmem, vmem, vmem, vmem, anyspace, anyspace],
+        in_specs=[anyspace, anyspace, anyspace, smem] + [anyspace] * 6,
         out_specs=(anyspace, vmem, vmem, vmem),
         scratch_shapes=[
+            pltpu.VMEM((KER, 1, D), f32),
+            pltpu.VMEM((1, D), f32),
+            pltpu.VMEM((1, D), f32),
+            pltpu.VMEM((1, D), f32),
             pltpu.VMEM((2, TOK, D), bf16),
             pltpu.VMEM((2, SEQ, HID), bf16),
             pltpu.VMEM((SEQ, D), bf16),
@@ -566,8 +567,11 @@
             pltpu.VMEM((2, 8, D), f32),
             pltpu.VMEM((16, D), f32),
             pltpu.VMEM((16, D), f32),
-            pltpu.VMEM((6, 8, D), f32),
-            pltpu.VMEM((5, 8, D), f32),
+            pltpu.VMEM((8, D), f32),
+            pltpu.VMEM((8, D), f32),
+            pltpu.VMEM((4, 8, D), f32),
+            pltpu.VMEM((4, 8, D), f32),
+            pltpu.VMEM((8, D), f32),
             pltpu.VMEM((1, HID), f32),
             pltpu.SemaphoreType.DMA((N_COPIES,)),
             pltpu.SemaphoreType.DMA((N_COPIES,)),

time: 93.3 us -> 89.9 us (0.964)
  Pallas kernels: 91.7 us -> 88.4 us
    pallas_call x1, Pallas kernels: 89.6 us -> 86.2 us  [per_device(): pl.pallas_call(kernel, out_shape=(jax.ShapeDtypeStruct((1, TOK, D), bf16)...]
where the time goes in v3:
time: 89.9 us; the launch traced here: 89.7 us
  Pallas kernels  88.4 us (98%)
  between operations  1.29 us (1%)
    pallas_call x1, Pallas kernels, per_device(): pl.pallas_call(kernel, out_shape=(jax.ShapeDtypeStruct((1, TOK, D), bf16)...  86.2 us
    pallas_call x1, Pallas kernels, per_device(): pl.pallas_call(deliver, out_shape=(jax.ShapeDtypeStruct((1, TOK, D), bf16...  2.17 us

profile of v3, /device:TPU:8, one launch (start us, length us, event | category | flops | bytes accessed | tf_op | source)
XLA Modules:
  0.0 89.7 jit_solution(14629532309872246097)
XLA Ops:
  1.3 86.2 %shard_map.145 = (bf16[1,128,1536]{2,1,0:T(8,128)(2,1)}, f32[96,768]{1,0:T(8,128)}, f32[96,768]{1,0:T(8,128)}, f32[16,1536]{1,0:T(8,128)}) custom-call(bf16[1,2,128,1536]{3,2,1,0:T(8,128)(2,1)} %x_hbm.1, bf16[1,2,512,768]{3,2,1,0:T(8,128)(2,1)} %h_hbm.1, bf16[1,128,1536]{2,1,0:T(8,128)(2,1)} %g_hbm.1, s32[1]{0:T(128)S(6)} %copy.16.plan_ref, ...), custom_call_target="tpu_custom_call" | custom-call | tf_op jit(solution)/shard_map/pallas_call | solution.py:526
  87.5 2.2 %shard_map.146 = (bf16[1,128,1536]{2,1,0:T(8,128)(2,1)}, f32[96,768]{1,0:T(8,128)}, f32[96,768]{1,0:T(8,128)}, f32[8,1536]{1,0:T(8,128)}, f32[3,1,1536]{2,1,0:T(1,128)}, /*index=5*/f32[1,3072]{1,0:T(1,128)}) custom-call(bf16[1,128,1536]{2,1,0:T(8,128)(2,1)} %get-tuple-element.16.gin, f32[96,768]{1,0:T(8,128)} %get-tuple-element.17.gwi, ...), custom_call_target="tpu_custom_call" | custom-call | tf_op jit(solution)/shard_map/pallas_call | solution.py:586

commit v4 on v3

--- a/solution.py
+++ b/solution.py
@@ -25,6 +25,7 @@
 YB = XB // 4
 WIDE = TOK + 16
 N_COPIES = 112
+CHUNKS = ((0, 256), (256, 512), (0, 512), (512, 256))
 N_LOCAL = 16
 
 
@@ -210,88 +211,106 @@
 
         lax.fori_loop(0, D // CH, block, 0)
 
-    def weight_part(c, k, src, hidden):
-        block = dot_tn(src[:, block_cols(k)], hidden[...]).astype(bf16)
-        part[c, k] = block[:, :CH]
-        part[c + 1, k] = block[:, CH:]
-
-    def ring_far(own, two, half, plus, minus):
-        far_a = remote(own.at[2, pl.ds(0, half)], two.at[0], plus)
-        far_b = remote(own.at[2, pl.ds(half, half)], two.at[1], minus)
+    def weight_part(m, k, src, hidden):
+        part[m, k] = dot_tn(src[:, block_cols(k)], hidden[...]).astype(bf16)
+
+    def ring_far(own, two, half, cols, plus, minus):
+        far_a = remote(own.at[2, pl.ds(0, half), cols], two.at[0, :, cols], plus)
+        far_b = remote(own.at[2, pl.ds(half, half), cols], two.at[1, :, cols], minus)
         return far_a, far_b
 
-    def ring_near(own, last, half, plus, minus):
-        near_b = remote(own.at[1, pl.ds(half, half)], last.at[0, pl.ds(half, half)], plus)
-        near_a = remote(own.at[3, pl.ds(0, half)], last.at[1, pl.ds(0, half)], minus)
+    def ring_near(own, last, half, cols, plus, minus):
+        low, high = pl.ds(0, half), pl.ds(half, half)
+        near_b = remote(own.at[1, high, cols], last.at[0, high, cols], plus)
+        near_a = remote(own.at[3, low, cols], last.at[1, low, cols], minus)
         return near_a, near_b
 
-    def ring_second(copies, own, two, last, half, plus, minus):
+    def ring_second(copies, own, two, last, half, cols, plus, minus):
         far_a, far_b, near_a, near_b = copies
+        low, high = pl.ds(0, half), pl.ds(half, half)
         far_a.wait_recv()
 
         def add_a(i, carry):
             rows = pl.ds(pl.multiple_of(i * 48, 16), 48)
-            own[1, rows, :] = (own[1, rows, :].astype(f32) + two[0, rows, :].astype(f32)).astype(bf16)
+            own[1, rows, cols] = (
+                own[1, rows, cols].astype(f32) + two[0, rows, cols].astype(f32)
+            ).astype(bf16)
             return carry
 
         lax.fori_loop(0, half // 48, add_a, 0)
-        sum_a = remote(own.at[1, pl.ds(0, half)], last.at[0, pl.ds(0, half)], plus)
+        sum_a = remote(own.at[1, low, cols], last.at[0, low, cols], plus)
         far_b.wait_recv()
 
         def add_b(i, carry):
             rows = pl.ds(pl.multiple_of(half + i * 48, 16), 48)
             here = pl.ds(pl.multiple_of(i * 48, 16), 48)
-            own[3, rows, :] = (own[3, rows, :].astype(f32) + two[1, here, :].astype(f32)).astype(bf16)
+            own[3, rows, cols] = (
+                own[3, rows, cols].astype(f32) + two[1, here, cols].astype(f32)
+            ).astype(bf16)
             return carry
 
         lax.fori_loop(0, half // 48, add_b, 0)
-        sum_b = remote(own.at[3, pl.ds(half, half)], last.at[1, pl.ds(half, half)], minus)
+        sum_b = remote(own.at[3, high, cols], last.at[1, high, cols], minus)
         return near_a, near_b, sum_a, sum_b
 
     x_copies, y_copies = {}, {}
 
+    def chunk(c):
+        return c // 2, pl.ds(*CHUNKS[c])
+
     def x_far(c):
-        x_copies[c] = ring_far(part.at[c], xr2.at[c], XB // 2, xp, xm)
+        m, cols = chunk(c)
+        x_copies[c] = ring_far(part.at[m], xr2.at[m], XB // 2, cols, xp, xm)
 
     def x_near(c):
-        x_copies[c] += ring_near(part.at[c], xrx.at[c], XB // 2, xp, xm)
+        m, cols = chunk(c)
+        x_copies[c] += ring_near(part.at[m], xrx.at[m], XB // 2, cols, xp, xm)
 
     def x_second(c):
-        x_copies[c] = ring_second(x_copies[c], part.at[c], xr2.at[c], xrx.at[c], XB // 2, xp, xm)
+        m, cols = chunk(c)
+        x_copies[c] = ring_second(
+            x_copies[c], part.at[m], xr2.at[m], xrx.at[m], XB // 2, cols, xp, xm
+        )
 
     def x_third(c):
+        m, cols = chunk(c)
         for copy in x_copies[c]:
             copy.wait_recv()
 
         def block(k, carry):
             for piece in range(2):
                 rows = pl.ds(pl.multiple_of(((yi + k) % 4) * YB + piece * 48, 16), 48)
-                q[c, k, pl.ds(piece * 48, 48), :] = (
-                    part[c, 0, rows, :].astype(f32)
-                    + xrx[c, 0, rows, :].astype(f32)
-                    + xrx[c, 1, rows, :].astype(f32)
+                q[m, k, pl.ds(piece * 48, 48), cols] = (
+                    part[m, 0, rows, cols].astype(f32)
+                    + xrx[m, 0, rows, cols].astype(f32)
+                    + xrx[m, 1, rows, cols].astype(f32)
                 ).astype(bf16)
             return carry
 
         lax.fori_loop(0, 4, block, 0)
 
     def y_first(c):
-        y_copies[c] = ring_far(q.at[c], yr2.at[c], YB // 2, yp, ym)
-        y_copies[c] += ring_near(q.at[c], yrx.at[c], YB // 2, yp, ym)
+        m, cols = chunk(c)
+        y_copies[c] = ring_far(q.at[m], yr2.at[m], YB // 2, cols, yp, ym)
+        y_copies[c] += ring_near(q.at[m], yrx.at[m], YB // 2, cols, yp, ym)
 
     def y_second(c):
-        y_copies[c] = ring_second(y_copies[c], q.at[c], yr2.at[c], yrx.at[c], YB // 2, yp, ym)
+        m, cols = chunk(c)
+        y_copies[c] = ring_second(
+            y_copies[c], q.at[m], yr2.at[m], yrx.at[m], YB // 2, cols, yp, ym
+        )
 
     def y_third(c):
+        m, cols = chunk(c)
         for copy in y_copies[c]:
             copy.wait_recv()
-        out = gwo_out if c < 2 else gwi_out
+        out = (gwo_out, gwi_out)[m]
         for piece in range(2):
             rows = pl.ds(piece * 48, 48)
-            out[rows, pl.ds((c % 2) * CH, CH)] = (
-                q[c, 0, rows, :].astype(f32)
-                + yrx[c, 0, rows, :].astype(f32)
-                + yrx[c, 1, rows, :].astype(f32)
+            out[rows, cols] = (
+                q[m, 0, rows, cols].astype(f32)
+                + yrx[m, 0, rows, cols].astype(f32)
+                + yrx[m, 1, rows, cols].astype(f32)
             )
 
     lg.wait()
@@ -369,18 +388,18 @@
     for k in order:
         s_core[k].wait_recv()
     s_pass[2].wait_recv()
-    weight_part(2, 2, sf, dh)
+    weight_part(1, 2, sf, dh)
     x_far(2)
     for k in order[1:]:
         s_pass[k] = pass_on(s_chip, sf, k)
     s_pass[1].wait_recv()
-    weight_part(2, 1, sf, dh)
+    weight_part(1, 1, sf, dh)
     s_pass[3].wait_recv()
-    weight_part(2, 3, sf, dh)
+    weight_part(1, 3, sf, dh)
     x_near(2)
     x_far(3)
     s_pass[0].wait_recv()
-    weight_part(2, 0, sf, dh)
+    weight_part(1, 0, sf, dh)
     x_third(0)
     y_first(0)
 
@@ -556,12 +575,12 @@
             pltpu.VMEM((2, WIDE, D), bf16),
             pltpu.VMEM((WIDE, D), bf16),
             pltpu.VMEM((WIDE, D), bf16),
-            pltpu.VMEM((4, 4, XB, CH), bf16),
-            pltpu.VMEM((4, 2, XB // 2, CH), bf16),
-            pltpu.VMEM((4, 2, XB, CH), bf16),
-            pltpu.VMEM((4, 4, YB, CH), bf16),
-            pltpu.VMEM((4, 2, YB // 2, CH), bf16),
-            pltpu.VMEM((4, 2, YB, CH), bf16),
+            pltpu.VMEM((2, 4, XB, HID), bf16),
+            pltpu.VMEM((2, 2, XB // 2, HID), bf16),
+            pltpu.VMEM((2, 2, XB, HID), bf16),
+            pltpu.VMEM((2, 4, YB, HID), bf16),
+            pltpu.VMEM((2, 2, YB // 2, HID), bf16),
+            pltpu.VMEM((2, 2, YB, HID), bf16),
             pltpu.VMEM((WIDE, D), f32),
             pltpu.VMEM((TOK, D), bf16),
             pltpu.VMEM((2, 8, D), f32),

time: 89.9 us -> 89.6 us (level)
  no operation moved by 1% of the time
where the time goes in v4:
time: 89.6 us; the launch traced here: 89.4 us
  Pallas kernels  88.1 us (98%)
  between operations  1.29 us (1%)
    pallas_call x1, Pallas kernels, per_device(): pl.pallas_call(kernel, out_shape=(jax.ShapeDtypeStruct((1, TOK, D), bf16)...  86 us
    pallas_call x1, Pallas kernels, per_device(): pl.pallas_call(deliver, out_shape=(jax.ShapeDtypeStruct((1, TOK, D), bf16...  2.17 us

profile of v4, /device:TPU:8, one launch (start us, length us, event | category | flops | bytes accessed | tf_op | source)
XLA Modules:
  0.0 89.4 jit_solution(1270397159708789231)
XLA Ops:
  1.3 86.0 %shard_map.145 = (bf16[1,128,1536]{2,1,0:T(8,128)(2,1)}, f32[96,768]{1,0:T(8,128)}, f32[96,768]{1,0:T(8,128)}, f32[16,1536]{1,0:T(8,128)}) custom-call(bf16[1,2,128,1536]{3,2,1,0:T(8,128)(2,1)} %x_hbm.1, bf16[1,2,512,768]{3,2,1,0:T(8,128)(2,1)} %h_hbm.1, bf16[1,128,1536]{2,1,0:T(8,128)(2,1)} %g_hbm.1, s32[1]{0:T(128)S(6)} %copy.16.plan_ref, ...), custom_call_target="tpu_custom_call" | custom-call | tf_op jit(solution)/shard_map/pallas_call | solution.py:545
  87.3 2.2 %shard_map.146 = (bf16[1,128,1536]{2,1,0:T(8,128)(2,1)}, f32[96,768]{1,0:T(8,128)}, f32[96,768]{1,0:T(8,128)}, f32[8,1536]{1,0:T(8,128)}, f32[3,1,1536]{2,1,0:T(1,128)}, /*index=5*/f32[1,3072]{1,0:T(1,128)}) custom-call(bf16[1,128,1536]{2,1,0:T(8,128)(2,1)} %get-tuple-element.16.gin, f32[96,768]{1,0:T(8,128)} %get-tuple-element.17.gwi, ...), custom_call_target="tpu_custom_call" | custom-call | tf_op jit(solution)/shard_map/pallas_call | solution.py:605

commit v5 on v4

--- a/solution.py
+++ b/solution.py
@@ -63,7 +63,8 @@
     seq_next, seq_prev = dev(t_=(t + 1) % 4), dev(t_=(t + 3) % 4)
     xp, xm = dev(dp_=((xi + 1) % 4) * 4 + yi), dev(dp_=((xi + 3) % 4) * 4 + yi)
     yp, ym = dev(dp_=xi * 4 + (yi + 1) % 4), dev(dp_=xi * 4 + (yi + 3) % 4)
-    x2, y2 = dev(dp_=((xi + 2) % 4) * 4 + yi), dev(dp_=xi * 4 + (yi + 2) % 4)
+    x2 = dev(dp_=((xi + 2) % 4) * 4 + yi)
+    y_a, y_b = dev(dp_=xi * 4 + yi + 1 - 2 * (yi % 2)), dev(dp_=xi * 4 + 3 - yi)
     z_down = dev(pz_=(pz + npipe - 1) % npipe)
     z_up = dev(pz_=(pz + 1) % npipe)
 
@@ -93,11 +94,11 @@
     own_rows = pl.ds(pl.multiple_of(t * TOK, TOK), TOK)
 
     barrier = pltpu.get_barrier_semaphore()
-    for to in (core_dev, chip_dev, diag_dev, xp, xm, x2, yp, ym, y2, z_down, z_up):
+    for to in (core_dev, chip_dev, diag_dev, xp, xm, x2, yp, ym, z_down, z_up):
         pl.semaphore_signal(barrier, inc=1, device_id=to, device_id_type=MESH)
     lx = local(x_hbm.at[0], xs)
     lh = local(h_hbm.at[0], hs)
-    pl.semaphore_wait(barrier, 11)
+    pl.semaphore_wait(barrier, 10)
 
     def block_cols(k):
         return pl.ds(pl.multiple_of(((xi + k) % 4) * XB, XB), XB)
@@ -504,21 +505,23 @@
     y_second(1)
     x_third(2)
     y_first(2)
-    y_third(1)
     for copy in a_x:
         copy.wait_recv()
-    ary[yi] = (arx[0] + arx[1]) + (arx[2] + arx[3])
-    a_y = [remote(ary.at[yi], ary.at[yi], to) for to in (yp, ym, y2)]
+    ary[0] = (arx[0] + arx[1]) + (arx[2] + arx[3])
+    a_y = remote(ary.at[0], ary.at[1], y_a)
+    y_third(1)
+    y_second(2)
+    a_y.wait_recv()
+    ary[2] = ary[0] + ary[1]
+    a_y = remote(ary.at[2], ary.at[3], y_b)
     x_third(3)
     y_first(3)
-    y_second(2)
-    for copy in a_y:
-        copy.wait_recv()
-    arf[...] = (ary[0] + ary[1]) + (ary[2] + ary[3])
+    y_third(2)
+    a_y.wait_recv()
+    arf[...] = ary[2] + ary[3]
     small_out[my8, :] = arf[...]
     a_back = remote(arf, small_out.at[my8], core_dev)
     y_second(3)
-    y_third(2)
     y_third(3)
     a_back.wait_recv()
     for copy in z_copies:

time: 89.6 us -> 90.2 us (level)
  the two profiles are of different devices: /device:TPU:8 before, /device:TPU:56 now
where the time goes in v5:
time: 90.2 us; the launch traced here: 90.1 us
  Pallas kernels  88.8 us (98%)
  between operations  1.29 us (1%)
    pallas_call x1, Pallas kernels, per_device(): pl.pallas_call(kernel, out_shape=(jax.ShapeDtypeStruct((1, TOK, D), bf16)...  86.6 us
    pallas_call x1, Pallas kernels, per_device(): pl.pallas_call(deliver, out_shape=(jax.ShapeDtypeStruct((1, TOK, D), bf16...  2.17 us

profile of v5, /device:TPU:56, one launch (start us, length us, event | category | flops | bytes accessed | tf_op | source)
XLA Modules:
  0.0 90.1 jit_solution(10201015868356390699)
XLA Ops:
  1.3 86.6 %shard_map.145 = (bf16[1,128,1536]{2,1,0:T(8,128)(2,1)}, f32[96,768]{1,0:T(8,128)}, f32[96,768]{1,0:T(8,128)}, f32[16,1536]{1,0:T(8,128)}) custom-call(bf16[1,2,128,1536]{3,2,1,0:T(8,128)(2,1)} %x_hbm.1, bf16[1,2,512,768]{3,2,1,0:T(8,128)(2,1)} %h_hbm.1, bf16[1,128,1536]{2,1,0:T(8,128)(2,1)} %g_hbm.1, s32[1]{0:T(128)S(6)} %copy.16.plan_ref, ...), custom_call_target="tpu_custom_call" | custom-call | tf_op jit(solution)/shard_map/pallas_call | solution.py:548
  87.9 2.2 %shard_map.146 = (bf16[1,128,1536]{2,1,0:T(8,128)(2,1)}, f32[96,768]{1,0:T(8,128)}, f32[96,768]{1,0:T(8,128)}, f32[8,1536]{1,0:T(8,128)}, f32[3,1,1536]{2,1,0:T(1,128)}, /*index=5*/f32[1,3072]{1,0:T(1,128)}) custom-call(bf16[1,128,1536]{2,1,0:T(8,128)(2,1)} %get-tuple-element.16.gin, f32[96,768]{1,0:T(8,128)} %get-tuple-element.17.gwi, ...), custom_call_target="tpu_custom_call" | custom-call | tf_op jit(solution)/shard_map/pallas_call | solution.py:608
